TPU v7x, 32 devices: a whole 2x2x4 slice. The times are simulated.
32 devices in a mesh: grp: 2 (over x), ta: 4 (over y, core), xyz: 4 (over z).
Axes of the slice: x: 2, y: 2, z: 4, core: 2. Of those that a mesh axis runs over, the one named last changes fastest.
Arguments:
- links: float32 [4, 3, 3, 2, 8, 4, 256], P(None, None, None, None, ('grp', 'ta'), 'xyz'), may hold values from -1 to 1, as said below
- momenta: float32 [4, 3, 3, 2, 8, 4, 256], P(None, None, None, None, ('grp', 'ta'), 'xyz'), may hold values from -11 to 11, as said below
- vectors: float32 [16, 3, 2, 2, 4, 4, 256], P('grp', None, None, None, 'ta', 'xyz'), may hold values from -6 to 6
- coefficients: float32 [4], replicated, may hold values from -1 to 1
Outputs:
- new_links: float32 [4, 3, 3, 2, 8, 4, 256], P(None, None, None, None, ('grp', 'ta'), 'xyz')
- new_momenta: float32 [4, 3, 3, 2, 8, 4, 256], P(None, None, None, None, ('grp', 'ta'), 'xyz')
- filtered: float32 [16, 3, 2, 2, 4, 4, 256], P('grp', None, None, None, 'ta', 'xyz')
Inputs may be any that keep to these rules, and one draw needn't show every extreme that they name: `links`: every 3 x 3 link matrix is special unitary up to rounding. `momenta`: every 3 x 3 momentum matrix is anti-Hermitian and traceless: an entry below the diagonal has exactly the negated real part and the same imaginary part as its mirror above, the diagonal has zero real parts.
All inputs are finite; a program needn't handle non-finite values.
Results may differ from a plain program's by a relative error of at most 0.0001.
Values sent between devices are 32-bit elements; how exact they have to be, the bound alone decides.
A program may use at most 64 MiB of HBM per device.

v0:
```python
import functools

import jax
import jax.numpy as jnp
from jax import lax
from jax.experimental import pallas as pl
from jax.experimental.pallas import tpu as pltpu
from jax.sharding import PartitionSpec as P

NZ = 32
NSTEP = 2
NCHEB = 3

coupling = 5.7
time_step = 0.1

LANES = 128
ROWS = 8
F32 = jnp.float32
UPPER = ((0, 1), (0, 2), (1, 2))


def iota(shape, dim):
    return lax.broadcasted_iota(jnp.int32, shape, len(shape) + dim)


def row_roll(values, count):
    count = count % 4
    if count == 0:
        return values
    return pltpu.roll(values, ROWS - 2 * count, axis=values.ndim - 2)


def swap_halves(values):
    axis = values.ndim - 2
    return jnp.where(
        iota(values.shape, -2) % 2 == 0,
        pltpu.roll(values, ROWS - 1, axis=axis),
        pltpu.roll(values, 1, axis=axis),
    )


def roll_y(values, amount):
    lane = iota(values.shape, -1)
    axis = values.ndim - 1
    if amount == 1:
        moved = pltpu.roll(values, LANES - NZ, axis=axis)
        return jnp.where(lane < LANES - NZ, moved, swap_halves(moved))
    moved = pltpu.roll(values, NZ, axis=axis)
    return jnp.where(lane >= NZ, moved, swap_halves(moved))


def roll_z(values, amount):
    position = iota(values.shape, -1) % NZ
    axis = values.ndim - 1
    if amount == 1:
        return jnp.where(
            position == NZ - 1,
            pltpu.roll(values, NZ - 1, axis=axis),
            pltpu.roll(values, LANES - 1, axis=axis),
        )
    return jnp.where(
        position == 0,
        pltpu.roll(values, LANES - NZ + 1, axis=axis),
        pltpu.roll(values, 1, axis=axis),
    )


def by_pair(choices):
    row = iota(choices[0].shape, -2)
    return jnp.where(
        row < 4,
        jnp.where(row < 2, choices[0], choices[1]),
        jnp.where(row < 6, choices[2], choices[3]),
    )


def product(left, right, left_h=False, right_h=False):
    real = imag = None
    for c in range(3):
        lr, li = (left[0, c], left[1, c]) if left_h else (left[0, :, c], left[1, :, c])
        rr, ri = (right[0, :, c], right[1, :, c]) if right_h else (right[0, c], right[1, c])
        lr, li, rr, ri = lr[:, None], li[:, None], rr[None], ri[None]
        both = lr * rr
        cross = li * ri
        first = lr * ri
        second = li * rr
        re = both + cross if left_h != right_h else both - cross
        if left_h and right_h:
            im = -first - second
        elif left_h:
            im = first - second
        elif right_h:
            im = second - first
        else:
            im = first + second
        real = re if real is None else real + re
        imag = im if imag is None else imag + im
    return jnp.stack([real, imag])


def traceless_part(m):
    parts = [0.5 * (m[0, i, j] - m[0, j, i]) for i, j in UPPER]
    parts += [0.5 * (m[1, i, j] + m[1, j, i]) for i, j in UPPER]
    trace = (m[1, 0, 0] + m[1, 1, 1] + m[1, 2, 2]) * (1.0 / 3.0)
    parts += [m[1, i, i] - trace for i in range(3)]
    return jnp.stack(parts)


def gauge_force(own, plus_t, plus_x, minus_t, minus_x, corner):
    ahead = [plus_t, plus_x, roll_y(own, 1), roll_z(own, 1)]
    behind = [minus_t, minus_x, roll_y(own, -1), roll_z(own, -1)]

    def slanted(arrays, k):
        return by_pair([arrays[(nu - k) % 4] for nu in range(4)])

    diagonal = slanted(behind, 0)
    turned = [
        by_pair([corner, corner, roll_y(plus_t, -1), roll_z(plus_t, -1)]),
        by_pair([corner, corner, roll_y(plus_x, -1), roll_z(plus_x, -1)]),
        roll_y(diagonal, 1),
        roll_z(diagonal, 1),
    ]
    staple = None
    for k in (1, 2, 3):
        up = product(
            product(row_roll(slanted(ahead, k), k), slanted(ahead, 4 - k), right_h=True),
            row_roll(own, k),
            right_h=True,
        )
        low = product(
            product(row_roll(slanted(turned, k), k), slanted(behind, 4 - k), True, True),
            row_roll(diagonal, k),
        )
        staple = up + low if staple is None else staple + up + low
    return (coupling / 3.0) * traceless_part(product(own, staple))


def third_row(two):
    re, im = [], []
    for colour in range(3):
        b, c = (colour + 1) % 3, (colour + 2) % 3
        ar, ai, dr, di = two[0, 0, b], two[1, 0, b], two[0, 1, c], two[1, 1, c]
        er, ei, fr, fi = two[0, 0, c], two[1, 0, c], two[0, 1, b], two[1, 1, b]
        re.append(ar * dr - ai * di - (er * fr - ei * fi))
        im.append(-(ar * di + ai * dr - (er * fi + ei * fr)))
    return jnp.stack([jnp.stack(re), jnp.stack(im)])


def evolve(moment, own):
    a = time_step * moment
    x01, x02, x12 = a[3], a[4], a[5]
    y01, y02, y12 = -a[0], -a[1], -a[2]
    h0, h1, h2 = a[6], a[7], a[8]
    n01 = x01 * x01 + y01 * y01
    n02 = x02 * x02 + y02 * y02
    n12 = x12 * x12 + y12 * y12
    g0 = h0 * h0 + n01 + n02
    g1 = h1 * h1 + n01 + n12
    g2 = h2 * h2 + n02 + n12
    u01 = (h0 + h1) * x01 + (x02 * x12 + y02 * y12)
    v01 = (h0 + h1) * y01 + (y02 * x12 - x02 * y12)
    p02 = x01 * x12 - y01 * y12
    q02 = x01 * y12 + y01 * x12
    u02 = (h0 + h2) * x02 + p02
    v02 = (h0 + h2) * y02 + q02
    u12 = (h1 + h2) * x12 + (x01 * x02 + y01 * y02)
    v12 = (h1 + h2) * y12 + (x01 * y02 - y01 * x02)
    s = 0.5 * (g0 + g1 + g2)
    d = (
        h0 * h1 * h2
        + 2.0 * (p02 * x02 + q02 * y02)
        - h0 * n12
        - h1 * n02
        - h2 * n01
    )
    c0r = 1.0 - d * d * (1.0 / 720.0)
    c0i = d * (s * (1.0 / 120.0) - 1.0 / 6.0)
    c1r = d * (1.0 / 24.0 - s * (1.0 / 360.0))
    c1i = 1.0 + s * (s * (1.0 / 120.0) - 1.0 / 6.0)
    c2r = s * (1.0 / 24.0 - s * (1.0 / 720.0)) - 0.5
    c2i = d * (1.0 / 120.0)
    re = [[None] * 3 for _ in range(3)]
    im = [[None] * 3 for _ in range(3)]
    for i, (h, g) in enumerate(((h0, g0), (h1, g1), (h2, g2))):
        re[i][i] = c0r + c1r * h + c2r * g
        im[i][i] = c0i + c1i * h + c2i * g
    for (i, j), x, y, u, v in (
        ((0, 1), x01, y01, u01, v01),
        ((0, 2), x02, y02, u02, v02),
        ((1, 2), x12, y12, u12, v12),
    ):
        rx = c1r * x + c2r * u
        iy = c1i * y + c2i * v
        ix = c1i * x + c2i * u
        ry = c1r * y + c2r * v
        re[i][j], re[j][i] = rx - iy, rx + iy
        im[i][j], im[j][i] = ix + ry, ix - ry
    e = jnp.stack([jnp.stack([jnp.stack(r) for r in re]), jnp.stack([jnp.stack(r) for r in im])])
    return product(e, own)


def spread(values, pair):
    return by_pair([row_roll(values, pair - p) for p in range(4)])


def matvec(matrix, v, herm=False):
    real = imag = None
    for c in range(3):
        mr, mi = (matrix[0, c], matrix[1, c]) if herm else (matrix[0, :, c], matrix[1, :, c])
        vr, vi = v[0, c][None], v[1, c][None]
        if herm:
            re = mr * vr + mi * vi
            im = mr * vi - mi * vr
        else:
            re = mr * vr - mi * vi
            im = mr * vi + mi * vr
        real = re if real is None else real + re
        imag = im if imag is None else imag + im
    return jnp.stack([real, imag])


def kernel(
    sizes,
    coef,
    u_ref,
    p_ref,
    mine_ref,
    give_ref,
    u_out,
    p_out,
    keep_out,
    back_out,
    state,
    pair_u,
    got_u,
    got_pair_u,
    send_p,
    pair_p,
    got_p,
    got_pair_p,
    hop_links,
    fields,
    got_fields,
    total,
    partial,
    got_back,
    send_sem,
    recv_sem,
):
    n_grp, n_ta, n_x = sizes
    grp, ta, x = lax.axis_index("grp"), lax.axis_index("ta"), lax.axis_index("xyz")
    n_t = n_grp * n_ta
    t = grp * n_ta + ta

    def device(dt, dx):
        tt = lax.rem(t + dt + n_t, n_t)
        return (tt // n_ta, lax.rem(tt, n_ta), lax.rem(x + dx + n_x, n_x))

    partner = (lax.rem(grp + 1, n_grp), ta, x)
    whole_to = [device(-1, 0), device(0, -1), device(1, 0), device(0, 1)]
    pair_to = [device(1, -1), device(-1, 1)]
    peers = whole_to + pair_to + [partner]
    barrier = pltpu.get_barrier_semaphore()
    for peer in peers:
        pl.semaphore_signal(
            barrier, inc=1, device_id=peer, device_id_type=pl.DeviceIdType.MESH
        )

    counter = [0]

    def copy(src, dst, to):
        n = counter[0]
        counter[0] += 1
        made = pltpu.make_async_remote_copy(
            src_ref=src,
            dst_ref=dst,
            send_sem=send_sem.at[n],
            recv_sem=recv_sem.at[n],
            device_id=to,
            device_id_type=pl.DeviceIdType.MESH,
        )
        made.start()
        return made

    pending = []

    pair_u[0] = u_ref[:, 0:2, :, 0:2, :]
    pair_u[1] = u_ref[:, 0:2, :, 2:4, :]
    state[0] = u_ref[...]
    pl.semaphore_wait(barrier, len(peers))

    first = [copy(u_ref.at[:, 0:2], got_u.at[i], whole_to[i]) for i in (1, 3, 0, 2)]
    first += [copy(pair_u.at[i], got_pair_u.at[i], pair_to[i]) for i in range(2)]
    give = copy(give_ref, fields.at[0, 2:4], partner)
    fields[0, 0:2] = mine_ref[...]
    pending += first + [give]
    for made in first:
        made.wait_recv()
    for i in range(4):
        state[i + 1, :, 0:2] = got_u[i]
        state[i + 1, :, 2] = third_row(got_u[i])
    low, high = got_pair_u[0], got_pair_u[1]
    both = jnp.concatenate([low, high, high, high], axis=3)
    state[5, :, 0:2] = both
    state[5, :, 2] = third_row(both)

    def force():
        return gauge_force(*[state[i] for i in range(6)])

    def send_moment(r, moment):
        send_p[r] = moment
        pair_p[r, 0] = moment[:, 0:2, :]
        pair_p[r, 1] = moment[:, 2:4, :]
        made = [copy(send_p.at[r], got_p.at[r, i], whole_to[i]) for i in (1, 3, 0, 2)]
        made += [copy(pair_p.at[r, i], got_pair_p.at[r, i], pair_to[i]) for i in range(2)]
        return made

    def send_fields(r):
        return [
            copy(fields.at[r], got_fields.at[r, 0], whole_to[1]),
            copy(fields.at[r], got_fields.at[r, 1], whole_to[3]),
        ]

    halo = None
    moment = p_ref[...] - (0.5 * time_step) * force()
    for r in range(NSTEP):
        made = send_moment(r, moment)
        pending += made
        if r == 0:
            give.wait_recv()
            halo = send_fields(0)
            pending += halo
        state[0] = evolve(moment, state[0])
        for one in made:
            one.wait_recv()

        @pl.loop(0, 4)
        def _(i):
            state[i + 1] = evolve(got_p[r, i], state[i + 1])

        low, high = got_pair_p[r, 0], got_pair_p[r, 1]
        state[5] = evolve(jnp.concatenate([low, high, high, high], axis=1), state[5])
        if r + 1 < NSTEP:
            moment = moment - time_step * force()

    own = state[0]
    u_out[...] = own
    backs = [state[4], roll_y(own, -1), roll_z(own, -1)]
    for i in range(3):
        hop_links[2 * i] = spread(own, i + 1)
        hop_links[2 * i + 1] = spread(backs[i], i + 1)

    def local_terms(k):
        @pl.loop(0, 4)
        def _(g):
            v = fields[k, g]
            acc = matvec(hop_links[2], roll_y(v, 1))
            acc = acc + matvec(hop_links[3], roll_y(v, -1), True)
            acc = acc + matvec(hop_links[4], roll_z(v, 1))
            partial[g] = acc + matvec(hop_links[5], roll_z(v, -1), True)

    def finish(k):
        scale = -1.0 / 6.0

        @pl.loop(0, 4)
        def _(g):
            acc = partial[g] + matvec(hop_links[0], got_fields[k, 0, g])
            acc = (acc + matvec(hop_links[1], got_fields[k, 1, g], True)) * scale
            if k == 0:
                fields[1, g] = acc
                total[g] = coef[0] * fields[0, g] + coef[1] * acc
            else:
                following = 2.0 * acc - fields[k - 1, g]
                if k + 1 < NCHEB:
                    fields[k + 1, g] = following
                total[g] = total[g] + coef[k + 1] * following

    for k in range(NCHEB):
        if k:
            halo = send_fields(k)
            pending += halo
        if k == 1:
            p_out[...] = moment - (0.5 * time_step) * force()
        local_terms(k)
        for one in halo:
            one.wait_recv()
        finish(k)
    back = copy(total.at[2:4], got_back, partner)
    keep_out[...] = total[0:2]
    back.wait_recv()
    back_out[...] = got_back[...]
    for one in pending + [back]:
        one.wait_send()


def body(sizes, links, momenta, vectors, coefficients):
    n_vec = vectors.shape[0]
    tiles = n_vec * 2 // ROWS
    u = links.reshape(4, 3, 3, 2, 2, LANES).transpose(3, 1, 2, 0, 4, 5)
    u = u.reshape(2, 3, 3, ROWS, LANES)
    m = momenta.reshape(4, 3, 3, 2, 2, LANES)
    p = jnp.stack(
        [m[:, i, j, 0] for i, j in UPPER]
        + [m[:, i, j, 1] for i, j in UPPER]
        + [m[:, i, i, 1] for i in range(3)]
    ).reshape(9, ROWS, LANES)
    v = vectors.reshape(tiles, 4, 3, 2, 2, 2, LANES).transpose(4, 0, 3, 2, 1, 5, 6)
    v = v.reshape(2, tiles, 2, 3, ROWS, LANES)
    low_half = lax.axis_index("grp") == 0
    mine = jnp.where(low_half, v[0], v[1])
    give = jnp.where(low_half, v[1], v[0])

    groups = 2 * tiles
    copies = 6 + 6 * NSTEP + 1 + 2 * NCHEB + 1
    vmem = pl.BlockSpec(memory_space=pltpu.VMEM)
    tile = (ROWS, LANES)
    new_u, new_p, keep, back = pl.pallas_call(
        functools.partial(kernel, sizes),
        out_shape=(
            jax.ShapeDtypeStruct((2, 3, 3) + tile, F32),
            jax.ShapeDtypeStruct((9,) + tile, F32),
            jax.ShapeDtypeStruct((tiles, 2, 3) + tile, F32),
            jax.ShapeDtypeStruct((tiles, 2, 3) + tile, F32),
        ),
        in_specs=[pl.BlockSpec(memory_space=pltpu.SMEM)] + [vmem] * 4,
        out_specs=(vmem,) * 4,
        scratch_shapes=[
            pltpu.VMEM((6, 2, 3, 3) + tile, F32),
            pltpu.VMEM((2, 2, 2, 3, 2, LANES), F32),
            pltpu.VMEM((4, 2, 2, 3) + tile, F32),
            pltpu.VMEM((2, 2, 2, 3, 2, LANES), F32),
            pltpu.VMEM((NSTEP, 9) + tile, F32),
            pltpu.VMEM((NSTEP, 2, 9, 2, LANES), F32),
            pltpu.VMEM((NSTEP, 4, 9) + tile, F32),
            pltpu.VMEM((NSTEP, 2, 9, 2, LANES), F32),
            pltpu.VMEM((6, 2, 3, 3) + tile, F32),
            pltpu.VMEM((NCHEB, groups, 2, 3) + tile, F32),
            pltpu.VMEM((NCHEB, 2, groups, 2, 3) + tile, F32),
            pltpu.VMEM((groups, 2, 3) + tile, F32),
            pltpu.VMEM((groups, 2, 3) + tile, F32),
            pltpu.VMEM((tiles, 2, 3) + tile, F32),
            pltpu.SemaphoreType.DMA((copies,)),
            pltpu.SemaphoreType.DMA((copies,)),
        ],
        compiler_params=pltpu.CompilerParams(
            collective_id=0, has_side_effects=True, vmem_limit_bytes=32 * 1024 * 1024
        ),
    )(coefficients, u, p, mine, give)

    new_links = new_u.reshape(2, 3, 3, 4, 2, LANES).transpose(3, 1, 2, 0, 4, 5)
    new_links = new_links.reshape(links.shape)
    q = new_p.reshape(9, 4, 2 * LANES)
    zero = jnp.zeros_like(q[0])
    where = {pair: n for n, pair in enumerate(UPPER)}
    entries = []
    for i in range(3):
        for j in range(3):
            if i == j:
                entries += [zero, q[6 + i]]
            elif i < j:
                entries += [q[where[i, j]], q[3 + where[i, j]]]
            else:
                entries += [-q[where[j, i]], q[3 + where[j, i]]]
    new_momenta = jnp.stack(entries, axis=1).reshape(momenta.shape)
    out = jnp.stack([jnp.where(low_half, keep, back), jnp.where(low_half, back, keep)])
    out = out.reshape(2, tiles, 2, 3, 4, 2, LANES).transpose(1, 4, 3, 2, 0, 5, 6)
    return new_links, new_momenta, out.reshape(vectors.shape)


def solution(mesh):
    sizes = (mesh.shape["grp"], mesh.shape["ta"], mesh.shape["xyz"])
    link_spec = P(None, None, None, None, ("grp", "ta"), "xyz", None)
    vector_spec = P("grp", None, None, None, "ta", "xyz", None)
    return jax.shard_map(
        functools.partial(body, sizes),
        mesh=mesh,
        in_specs=(link_spec, link_spec, vector_spec, P()),
        out_specs=(link_spec, link_spec, vector_spec),
        check_vma=False,
    )
```

profile of v0, /device:TPU:0, one launch (start us, length us, event | category | flops | bytes accessed | tf_op | source)
XLA Modules:
  0.0 46.4 jit_solution(15541514974617427095)
XLA Ops:
  0.6 0.0 copy-start.1
  0.6 0.8 %fusion = (f32[4,1,1,1,2,128]{5,4,3,2,1,0:T(2,128)S(1)}, f32[4,1,1,1,2,128]{5,4,3,2,1,0:T(2,128)S(1)}, f32[4,1,1,1,2,128]{5,4,3,2,1,0:T(2,128)S(1)}, f32[4,1,1,1...) fusion(f32[4,3,3,2,2,128]{5,4,3,2,1,0:T(2,128)} %bitcast.60), kind=kLoop, calls=%fused_computation.33 | loop fusion | bytes 73728 | tf_op jit(solution)/shard_map/slice | solution.py:406
  1.6 0.0 copy-done.1
  1.6 0.0 copy-start.2
  1.7 0.8 %copy-done.2 = f32[4,3,3,2,1,1,256]{6,5,4,3,2,1,0:T(1,128)S(1)} copy-done((f32[4,3,3,2,1,1,256]{6,5,4,3,2,1,0:T(1,128)S(1)}, f32[4,3,3,2,1,1,256]{6,5,4,3,2,1,0:T(1,128)}, u32[]{:S(2)}) %copy-start.2) | copy-done | bytes 73752
  2.5 0.0 copy-start
  2.6 0.6 %copy-done = f32[4]{0:T(128)S(1)} copy-done((f32[4]{0:T(128)S(1)}, f32[4]{0:T(128)}, u32[]{:S(2)}) %copy-start) | copy-done | bytes 40
  3.2 40.8 %shard_map.67 = (f32[2,3,3,8,128]{4,3,2,1,0:T(8,128)S(1)}, f32[9,8,128]{2,1,0:T(8,128)S(1)}, f32[2,2,3,8,128]{4,3,2,1,0:T(8,128)S(1)}, f32[2,2,3,8,128]{4,3,2,1,0:T(8,128)S(1)}) custom-call(f32[4]{0:T(128)S(1)} %copy-done, f32[2,3,3,8,128]{4,3,2,1,0:T(8,128)S(1)} %bitcast.48, f32[9,8,128]{2,1,0:T(8,128)S(1)} %constant_dynamic-update-slice_fusion.p_ref, ...), custom_call_target="tpu_custom_call" | custom-call | tf_op jit(solution)/shard_map/pallas_call | solution.py:418
  44.1 0.7 %copy.33 = f32[2,4,3,2,2,2,128]{6,5,4,3,2,1,0:T(2,128)} copy(f32[2,4,3,2,2,2,128]{6,5,1,2,3,0,4:T(2,128)S(1)} %maximum_bitcast_fusion) | data formatting | bytes 196608 | tf_op jit(solution)/shard_map/transpose | solution.py:467
  45.1 0.7 %copy.34 = f32[4,3,3,2,1,1,256]{6,5,4,3,2,1,0:T(1,128)} copy(f32[4,3,3,2,1,1,256]{6,0,3,2,1,5,4:T(4,128)S(1)} %bitcast.57) | data formatting | bytes 147456
  45.8 0.7 %copy.32 = f32[4,3,3,2,2,128]{5,4,3,2,1,0:T(2,128)} copy(f32[4,3,3,2,2,128]{5,4,0,2,1,3:T(2,128)S(1)} %bitcast.51) | data formatting | bytes 147456 | tf_op jit(solution)/shard_map/transpose | solution.py:451
  (42 shorter events, 0.4 us)
Async XLA Ops:
  0.6 1.0 %copy-start.1 = (f32[8,3,2,2,1,1,256]{6,5,4,3,2,1,0:T(1,128)S(1)}, f32[8,3,2,2,1,1,256]{6,5,4,3,2,1,0:T(1,128)}, u32[]{:S(2)}) copy-start(f32[8,3,2,2,1,1,256]{6,5,4,3,2,1,0:T(1,128)} %param.6) | copy-start | bytes 294916
  1.6 0.9 %copy-start.2 = (f32[4,3,3,2,1,1,256]{6,5,4,3,2,1,0:T(1,128)S(1)}, f32[4,3,3,2,1,1,256]{6,5,4,3,2,1,0:T(1,128)}, u32[]{:S(2)}) copy-start(f32[4,3,3,2,1,1,256]{6,5,4,3,2,1,0:T(1,128)} %param.4) | copy-start | bytes 221188
  2.5 0.7 %copy-start = (f32[4]{0:T(128)S(1)}, f32[4]{0:T(128)}, u32[]{:S(2)}) copy-start(f32[4]{0:T(128)} %coef.1) | copy-start | bytes 52
where the time goes:
time: 46.6 us; the launch traced here: 46.4 us
  Pallas kernels  40.8 us (88%)
  local copies, waits for them, and re-layouts  4.68 us (10%)
  between operations  0.85 us (2%)
    pallas_call x1, Pallas kernels, body(): pl.pallas_call(functools.partial(kernel, sizes), out_shape=(jax.ShapeDtyp...  40.8 us
    unnamed x29, local copies, waits for them, and re-layouts  2.34 us

commit v1 on v0

--- a/solution.py
+++ b/solution.py
@@ -220,17 +220,49 @@
     return jnp.stack([real, imag])
 
 
+def site_links(own):
+    return [
+        spread(own, 1),
+        spread(own, 2),
+        spread(roll_y(own, -1), 2),
+        spread(own, 3),
+        spread(roll_z(own, -1), 3),
+    ]
+
+
+def gather_rows(ref, starts):
+    return jnp.concatenate([ref[pl.ds(s, 2), :] for s in starts], axis=0)
+
+
+def scatter_rows(ref, starts, values):
+    for n, s in enumerate(starts):
+        ref[pl.ds(s, 2), :] = values[2 * n : 2 * n + 2]
+
+
+def link_rows(i, j, c):
+    return [(((mu * 3 + i) * 3 + j) * 2 + c) * 2 for mu in range(4)]
+
+
+def vector_rows(tile, a, c, h):
+    return [((((4 * tile + n) * 3 + a) * 2 + c) * 2 + h) * 2 for n in range(4)]
+
+
 def kernel(
     sizes,
+    tiles,
     coef,
-    u_ref,
-    p_ref,
-    mine_ref,
-    give_ref,
-    u_out,
-    p_out,
-    keep_out,
-    back_out,
+    links_ref,
+    momenta_ref,
+    vectors_ref,
+    links_out,
+    momenta_out,
+    vectors_out,
+    links_in,
+    momenta_in,
+    vectors_in,
+    two_rows,
+    v_in,
+    v_done,
     state,
     pair_u,
     got_u,
@@ -244,11 +276,12 @@
     got_fields,
     total,
     partial,
-    got_back,
+    load_sem,
     send_sem,
     recv_sem,
 ):
     n_grp, n_ta, n_x = sizes
+    ring = n_grp * tiles == n_x and n_x == 4
     grp, ta, x = lax.axis_index("grp"), lax.axis_index("ta"), lax.axis_index("xyz")
     n_t = n_grp * n_ta
     t = grp * n_ta + ta
@@ -257,46 +290,115 @@
         tt = lax.rem(t + dt + n_t, n_t)
         return (tt // n_ta, lax.rem(tt, n_ta), lax.rem(x + dx + n_x, n_x))
 
-    partner = (lax.rem(grp + 1, n_grp), ta, x)
+    def beside(dg, dx):
+        return (lax.rem(grp + dg, n_grp), ta, lax.rem(x + dx, n_x))
+
     whole_to = [device(-1, 0), device(0, -1), device(1, 0), device(0, 1)]
     pair_to = [device(1, -1), device(-1, 1)]
-    peers = whole_to + pair_to + [partner]
+    if ring:
+        whole_to.append(device(0, 2))
+        peers = [device(-1, 0), device(1, 0)] + pair_to
+        peers += [beside(dg, dx) for dg in range(n_grp) for dx in range(n_x) if dg or dx]
+    else:
+        peers = whole_to + pair_to + [beside(1, 0)]
     barrier = pltpu.get_barrier_semaphore()
     for peer in peers:
         pl.semaphore_signal(
             barrier, inc=1, device_id=peer, device_id_type=pl.DeviceIdType.MESH
         )
+    loads = [
+        pltpu.make_async_copy(links_ref, links_in, load_sem.at[0]),
+        pltpu.make_async_copy(vectors_ref, vectors_in, load_sem.at[1]),
+        pltpu.make_async_copy(momenta_ref, momenta_in, load_sem.at[2]),
+    ]
+    for load in loads:
+        load.start()
 
     counter = [0]
 
-    def copy(src, dst, to):
-        n = counter[0]
-        counter[0] += 1
-        made = pltpu.make_async_remote_copy(
+    def describe(src, dst, to, send, recv):
+        return pltpu.make_async_remote_copy(
             src_ref=src,
             dst_ref=dst,
-            send_sem=send_sem.at[n],
-            recv_sem=recv_sem.at[n],
+            send_sem=send_sem.at[send],
+            recv_sem=recv_sem.at[recv],
             device_id=to,
             device_id_type=pl.DeviceIdType.MESH,
         )
+
+    def take(count):
+        counter[0] += count
+        return counter[0] - count
+
+    def copy(src, dst, to):
+        n = take(1)
+        made = describe(src, dst, to, n, n)
         made.start()
         return made
 
     pending = []
 
-    pair_u[0] = u_ref[:, 0:2, :, 0:2, :]
-    pair_u[1] = u_ref[:, 0:2, :, 2:4, :]
-    state[0] = u_ref[...]
+    loads[0].wait()
+    for i in range(3):
+        for j in range(3):
+            for c in range(2):
+                state[0, c, i, j] = gather_rows(links_in, link_rows(i, j, c))
+    two_rows[...] = state[0, :, 0:2]
+    pair_u[0] = two_rows[:, :, :, 0:2, :]
+    pair_u[1] = two_rows[:, :, :, 2:4, :]
     pl.semaphore_wait(barrier, len(peers))
 
-    first = [copy(u_ref.at[:, 0:2], got_u.at[i], whole_to[i]) for i in (1, 3, 0, 2)]
+    first = [copy(two_rows, got_u.at[i], whole_to[i]) for i in (1, 3, 0, 2)]
     first += [copy(pair_u.at[i], got_pair_u.at[i], pair_to[i]) for i in range(2)]
-    give = copy(give_ref, fields.at[0, 2:4], partner)
-    fields[0, 0:2] = mine_ref[...]
-    pending += first + [give]
+    pending += first
+
+    loads[1].wait()
+    for h in range(2):
+        for tile in range(tiles):
+            for c in range(2):
+                for a in range(3):
+                    v_in[h, tile, c, a] = gather_rows(vectors_in, vector_rows(tile, a, c, h))
+    loads[2].wait()
+    moment = jnp.stack(
+        [gather_rows(momenta_in, link_rows(i, j, 0)) for i, j in UPPER]
+        + [gather_rows(momenta_in, link_rows(i, j, 1)) for i, j in UPPER]
+        + [gather_rows(momenta_in, link_rows(i, i, 1)) for i in range(3)]
+    )
+    send_p[0] = moment
     for made in first:
         made.wait_recv()
+
+    if ring:
+        far = copy(two_rows, got_u.at[4], whole_to[4])
+        pending.append(far)
+        own_tile = x // tiles
+        home = lax.rem(x, tiles)
+        out_send, out_recv = take(2 * tiles), take(n_x)
+        moves = []
+        for h in range(2):
+            for tile in range(tiles):
+                target = grp * tiles + tile
+                slot = lax.rem(x - target + n_x, n_x)
+                here = jnp.logical_and(grp == h, x == target)
+                made = describe(
+                    v_in.at[h, tile],
+                    fields.at[0, slot],
+                    (h, ta, target),
+                    out_send + h * tiles + tile,
+                    out_recv + slot,
+                )
+                moves.append((here, made))
+                pl.when(jnp.logical_not(here))(made.start)
+
+        @pl.when(own_tile == grp)
+        def _():
+            fields[0, 0] = v_in[grp, home]
+
+    else:
+        give = copy(v_in.at[1 - grp], fields.at[0, tiles : 2 * tiles], beside(1, 0))
+        fields[0, 0:tiles] = v_in[grp]
+        pending.append(give)
+
     for i in range(4):
         state[i + 1, :, 0:2] = got_u[i]
         state[i + 1, :, 2] = third_row(got_u[i])
@@ -314,6 +416,8 @@
         pair_p[r, 1] = moment[:, 2:4, :]
         made = [copy(send_p.at[r], got_p.at[r, i], whole_to[i]) for i in (1, 3, 0, 2)]
         made += [copy(pair_p.at[r, i], got_pair_p.at[r, i], pair_to[i]) for i in range(2)]
+        if ring:
+            made.append(copy(send_p.at[r], got_p.at[r, 4], whole_to[4]))
         return made
 
     def send_fields(r):
@@ -323,15 +427,24 @@
         ]
 
     halo = None
-    moment = p_ref[...] - (0.5 * time_step) * force()
+    last = []
+    moment = send_p[0] - (0.5 * time_step) * force()
     for r in range(NSTEP):
         made = send_moment(r, moment)
         pending += made
-        if r == 0:
+        if ring:
+            last.append(made.pop())
+        elif r == 0:
             give.wait_recv()
             halo = send_fields(0)
             pending += halo
         state[0] = evolve(moment, state[0])
+        if ring and r == 1:
+            far.wait_recv()
+            state[6, :, 0:2] = got_u[4]
+            state[6, :, 2] = third_row(got_u[4])
+            last[0].wait_recv()
+            state[6] = evolve(got_p[0, 4], state[6])
         for one in made:
             one.wait_recv()
 
@@ -344,128 +457,211 @@
         if r + 1 < NSTEP:
             moment = moment - time_step * force()
 
-    own = state[0]
-    u_out[...] = own
-    backs = [state[4], roll_y(own, -1), roll_z(own, -1)]
-    for i in range(3):
-        hop_links[2 * i] = spread(own, i + 1)
-        hop_links[2 * i + 1] = spread(backs[i], i + 1)
-
-    def local_terms(k):
-        @pl.loop(0, 4)
-        def _(g):
-            v = fields[k, g]
-            acc = matvec(hop_links[2], roll_y(v, 1))
-            acc = acc + matvec(hop_links[3], roll_y(v, -1), True)
-            acc = acc + matvec(hop_links[4], roll_z(v, 1))
-            partial[g] = acc + matvec(hop_links[5], roll_z(v, -1), True)
-
-    def finish(k):
-        scale = -1.0 / 6.0
-
-        @pl.loop(0, 4)
-        def _(g):
-            acc = partial[g] + matvec(hop_links[0], got_fields[k, 0, g])
-            acc = (acc + matvec(hop_links[1], got_fields[k, 1, g], True)) * scale
-            if k == 0:
-                fields[1, g] = acc
-                total[g] = coef[0] * fields[0, g] + coef[1] * acc
+    def finish_momenta():
+        done = moment - (0.5 * time_step) * force()
+        zero = jnp.zeros_like(done[0])
+        for n, (i, j) in enumerate(UPPER):
+            scatter_rows(momenta_out, link_rows(i, j, 0), done[n])
+            scatter_rows(momenta_out, link_rows(j, i, 0), -done[n])
+            scatter_rows(momenta_out, link_rows(i, j, 1), done[n + 3])
+            scatter_rows(momenta_out, link_rows(j, i, 1), done[n + 3])
+        for i in range(3):
+            scatter_rows(momenta_out, link_rows(i, i, 0), zero)
+            scatter_rows(momenta_out, link_rows(i, i, 1), done[6 + i])
+
+    def finish_links():
+        for i in range(3):
+            for j in range(3):
+                for c in range(2):
+                    scatter_rows(links_out, link_rows(i, j, c), state[0, c, i, j])
+
+    def step(k, g, acc):
+        acc = acc * (-1.0 / 6.0)
+        if k == 0:
+            fields[1, g] = acc
+            total[g] = coef[0] * fields[0, g] + coef[1] * acc
+        else:
+            following = 2.0 * acc - fields[k - 1, g]
+            if k + 1 < NCHEB:
+                fields[k + 1, g] = following
+            total[g] = total[g] + coef[k + 1] * following
+
+    def hop_local(k, g, at):
+        v = fields[k, g]
+        acc = matvec(hop_links[at, 1], roll_y(v, 1))
+        acc = acc + matvec(hop_links[at, 2], roll_y(v, -1), True)
+        acc = acc + matvec(hop_links[at, 3], roll_z(v, 1))
+        return acc + matvec(hop_links[at, 4], roll_z(v, -1), True)
+
+    def store_links(at, slot):
+        for n, matrix in enumerate(site_links(state[slot])):
+            hop_links[at, n] = matrix
+
+    if ring:
+        for at, slot in ((0, 0), (1, 2), (3, 4)):
+            store_links(at, slot)
+        last[1].wait_recv()
+        state[6] = evolve(got_p[1, 4], state[6])
+        store_links(2, 6)
+        for slot in range(n_x):
+            waiter = describe(v_in.at[0, 0], fields.at[0, slot], beside(1, 0), 0, out_recv + slot)
+            if slot:
+                waiter.wait_recv()
             else:
-                following = 2.0 * acc - fields[k - 1, g]
-                if k + 1 < NCHEB:
-                    fields[k + 1, g] = following
-                total[g] = total[g] + coef[k + 1] * following
-
-    for k in range(NCHEB):
-        if k:
-            halo = send_fields(k)
-            pending += halo
-        if k == 1:
-            p_out[...] = moment - (0.5 * time_step) * force()
-        local_terms(k)
-        for one in halo:
-            one.wait_recv()
-        finish(k)
-    back = copy(total.at[2:4], got_back, partner)
-    keep_out[...] = total[0:2]
-    back.wait_recv()
-    back_out[...] = got_back[...]
-    for one in pending + [back]:
+                pl.when(own_tile != grp)(waiter.wait_recv)
+
+        def hop(k, g):
+            after, before = (g + 1) % n_x, (g + n_x - 1) % n_x
+            acc = hop_local(k, g, g)
+            acc = acc + matvec(hop_links[g, 0], fields[k, after])
+            acc = acc + matvec(hop_links[before, 0], fields[k, before], True)
+            step(k, g, acc)
+
+        for k in range(NCHEB - 1):
+
+            @pl.loop(0, n_x)
+            def _(g):
+                after, before = lax.rem(g + 1, n_x), lax.rem(g + n_x - 1, n_x)
+                acc = hop_local(k, g, g)
+                acc = acc + matvec(hop_links[g, 0], fields[k, after])
+                acc = acc + matvec(hop_links[before, 0], fields[k, before], True)
+                step(k, g, acc)
+
+        back_send, back_recv = take(n_x), take(2 * tiles)
+        backs = []
+        for g in (2, 1, 3, 0):
+            hop(NCHEB - 1, g)
+            made = describe(
+                total.at[g],
+                v_done.at[grp, home],
+                (own_tile, ta, lax.rem(x + g, n_x)),
+                back_send + g,
+                back_recv + grp * tiles + home,
+            )
+            backs.append((g, made))
+            if g:
+                made.start()
+            else:
+                pl.when(own_tile != grp)(made.start)
+
+        @pl.when(own_tile == grp)
+        def _():
+            v_done[grp, home] = total[0]
+
+        finish_momenta()
+        finish_links()
+        for h in range(2):
+            for tile in range(tiles):
+                here, _ = moves[h * tiles + tile]
+                waiter = describe(
+                    total.at[0],
+                    v_done.at[h, tile],
+                    beside(1, 0),
+                    0,
+                    back_recv + h * tiles + tile,
+                )
+                pl.when(jnp.logical_not(here))(waiter.wait_recv)
+        for here, made in moves:
+            pl.when(jnp.logical_not(here))(made.wait_send)
+        for g, made in backs:
+            if g:
+                made.wait_send()
+            else:
+                pl.when(own_tile != grp)(made.wait_send)
+    else:
+        store_links(0, 0)
+        hop_links[1, 0] = spread(state[4], 1)
+        finish_links()
+        for k in range(NCHEB):
+            if k:
+                halo = send_fields(k)
+                pending += halo
+            if k == 1:
+                finish_momenta()
+
+            @pl.loop(0, 2 * tiles)
+            def _(g):
+                partial[g] = hop_local(k, g, 0)
+
+            for one in halo:
+                one.wait_recv()
+
+            @pl.loop(0, 2 * tiles)
+            def _(g):
+                acc = partial[g] + matvec(hop_links[0, 0], got_fields[k, 0, g])
+                acc = acc + matvec(hop_links[1, 0], got_fields[k, 1, g], True)
+                step(k, g, acc)
+
+        back = copy(total.at[tiles : 2 * tiles], v_done.at[grp], beside(1, 0))
+        v_done[grp] = total[0:tiles]
+        back.wait_recv()
+        pending.append(back)
+
+    for h in range(2):
+        for tile in range(tiles):
+            for c in range(2):
+                for a in range(3):
+                    scatter_rows(vectors_out, vector_rows(tile, a, c, h), v_done[h, tile, c, a])
+    for one in pending:
         one.wait_send()
 
 
 def body(sizes, links, momenta, vectors, coefficients):
-    n_vec = vectors.shape[0]
-    tiles = n_vec * 2 // ROWS
-    u = links.reshape(4, 3, 3, 2, 2, LANES).transpose(3, 1, 2, 0, 4, 5)
-    u = u.reshape(2, 3, 3, ROWS, LANES)
-    m = momenta.reshape(4, 3, 3, 2, 2, LANES)
-    p = jnp.stack(
-        [m[:, i, j, 0] for i, j in UPPER]
-        + [m[:, i, j, 1] for i, j in UPPER]
-        + [m[:, i, i, 1] for i in range(3)]
-    ).reshape(9, ROWS, LANES)
-    v = vectors.reshape(tiles, 4, 3, 2, 2, 2, LANES).transpose(4, 0, 3, 2, 1, 5, 6)
-    v = v.reshape(2, tiles, 2, 3, ROWS, LANES)
-    low_half = lax.axis_index("grp") == 0
-    mine = jnp.where(low_half, v[0], v[1])
-    give = jnp.where(low_half, v[1], v[0])
-
+    tiles = vectors.shape[0] * 2 // ROWS
     groups = 2 * tiles
-    copies = 6 + 6 * NSTEP + 1 + 2 * NCHEB + 1
+    copies = 2 * (groups + 4) + 7 + 7 * NSTEP + 2 * NCHEB + 2
     vmem = pl.BlockSpec(memory_space=pltpu.VMEM)
+    hbm = pl.BlockSpec(memory_space=pltpu.HBM)
     tile = (ROWS, LANES)
-    new_u, new_p, keep, back = pl.pallas_call(
-        functools.partial(kernel, sizes),
+    flat_links = (links.size // LANES, LANES)
+    flat_vectors = (vectors.size // LANES, LANES)
+    new_links, new_momenta, filtered = pl.pallas_call(
+        functools.partial(kernel, sizes, tiles),
         out_shape=(
-            jax.ShapeDtypeStruct((2, 3, 3) + tile, F32),
-            jax.ShapeDtypeStruct((9,) + tile, F32),
-            jax.ShapeDtypeStruct((tiles, 2, 3) + tile, F32),
-            jax.ShapeDtypeStruct((tiles, 2, 3) + tile, F32),
+            jax.ShapeDtypeStruct(flat_links, F32),
+            jax.ShapeDtypeStruct(flat_links, F32),
+            jax.ShapeDtypeStruct(flat_vectors, F32),
         ),
-        in_specs=[pl.BlockSpec(memory_space=pltpu.SMEM)] + [vmem] * 4,
-        out_specs=(vmem,) * 4,
+        in_specs=[pl.BlockSpec(memory_space=pltpu.SMEM)] + [hbm] * 3,
+        out_specs=(vmem,) * 3,
         scratch_shapes=[
-            pltpu.VMEM((6, 2, 3, 3) + tile, F32),
+            pltpu.VMEM(flat_links, F32),
+            pltpu.VMEM(flat_links, F32),
+            pltpu.VMEM(flat_vectors, F32),
+            pltpu.VMEM((2, 2, 3) + tile, F32),
+            pltpu.VMEM((2, tiles, 2, 3) + tile, F32),
+            pltpu.VMEM((2, tiles, 2, 3) + tile, F32),
+            pltpu.VMEM((7, 2, 3, 3) + tile, F32),
             pltpu.VMEM((2, 2, 2, 3, 2, LANES), F32),
-            pltpu.VMEM((4, 2, 2, 3) + tile, F32),
+            pltpu.VMEM((5, 2, 2, 3) + tile, F32),
             pltpu.VMEM((2, 2, 2, 3, 2, LANES), F32),
             pltpu.VMEM((NSTEP, 9) + tile, F32),
             pltpu.VMEM((NSTEP, 2, 9, 2, LANES), F32),
-            pltpu.VMEM((NSTEP, 4, 9) + tile, F32),
+            pltpu.VMEM((NSTEP, 5, 9) + tile, F32),
             pltpu.VMEM((NSTEP, 2, 9, 2, LANES), F32),
-            pltpu.VMEM((6, 2, 3, 3) + tile, F32),
+            pltpu.VMEM((4, 5, 2, 3, 3) + tile, F32),
             pltpu.VMEM((NCHEB, groups, 2, 3) + tile, F32),
             pltpu.VMEM((NCHEB, 2, groups, 2, 3) + tile, F32),
             pltpu.VMEM((groups, 2, 3) + tile, F32),
             pltpu.VMEM((groups, 2, 3) + tile, F32),
-            pltpu.VMEM((tiles, 2, 3) + tile, F32),
+            pltpu.SemaphoreType.DMA((3,)),
             pltpu.SemaphoreType.DMA((copies,)),
             pltpu.SemaphoreType.DMA((copies,)),
         ],
         compiler_params=pltpu.CompilerParams(
-            collective_id=0, has_side_effects=True, vmem_limit_bytes=32 * 1024 * 1024
+            collective_id=0, has_side_effects=True, vmem_limit_bytes=60 * 1024 * 1024
         ),
-    )(coefficients, u, p, mine, give)
-
-    new_links = new_u.reshape(2, 3, 3, 4, 2, LANES).transpose(3, 1, 2, 0, 4, 5)
-    new_links = new_links.reshape(links.shape)
-    q = new_p.reshape(9, 4, 2 * LANES)
-    zero = jnp.zeros_like(q[0])
-    where = {pair: n for n, pair in enumerate(UPPER)}
-    entries = []
-    for i in range(3):
-        for j in range(3):
-            if i == j:
-                entries += [zero, q[6 + i]]
-            elif i < j:
-                entries += [q[where[i, j]], q[3 + where[i, j]]]
-            else:
-                entries += [-q[where[j, i]], q[3 + where[j, i]]]
-    new_momenta = jnp.stack(entries, axis=1).reshape(momenta.shape)
-    out = jnp.stack([jnp.where(low_half, keep, back), jnp.where(low_half, back, keep)])
-    out = out.reshape(2, tiles, 2, 3, 4, 2, LANES).transpose(1, 4, 3, 2, 0, 5, 6)
-    return new_links, new_momenta, out.reshape(vectors.shape)
+    )(
+        coefficients,
+        links.reshape(flat_links),
+        momenta.reshape(flat_links),
+        vectors.reshape(flat_vectors),
+    )
+    return (
+        new_links.reshape(links.shape),
+        new_momenta.reshape(momenta.shape),
+        filtered.reshape(vectors.shape),
+    )
 
 
 def solution(mesh):

time: 46.6 us -> 39.8 us (0.85)
  Pallas kernels: 40.8 us -> 35.8 us
  local copies, waits for them, and re-layouts: 4.68 us -> 3.12 us
    pallas_call x1, Pallas kernels: 40.8 us -> 35.8 us  [body(): pl.pallas_call(functools.partial(kernel, sizes, tiles), out_shape=(jax.Sh...]
    transpose x2 -> x0, local copies, waits for them, and re-layouts: 1.33 us -> none  [the longest x1 0.68 us: body(): out.reshape(2, tiles, 2, 3, 4, 2, LANES).transpose(1, 4, 3, 2, 0, 5, 6)]
    slice x2 -> x0, local copies, waits for them, and re-layouts: 0.85 us -> none  [the longest x1 0.85 us: body(): m[:, i, i, 1]]
    unnamed x29 -> x7, local copies, waits for them, and re-layouts: 2.34 us -> 3.12 us
where the time goes in v1:
time: 39.8 us; the launch traced here: 39.6 us
  Pallas kernels  35.8 us (90%)
  local copies, waits for them, and re-layouts  3.12 us (8%)
  between operations  0.65 us (2%)
    pallas_call x1, Pallas kernels, body(): pl.pallas_call(functools.partial(kernel, sizes, tiles), out_shape=(jax.Sh...  35.8 us
    unnamed x7, local copies, waits for them, and re-layouts  3.12 us

profile of v1, /device:TPU:0, one launch (start us, length us, event | category | flops | bytes accessed | tf_op | source)
XLA Modules:
  0.0 39.6 jit_solution(2170669220402687248)
XLA Ops:
  0.6 35.8 %shard_map.67 = (f32[144,128]{1,0:T(8,128)}, f32[144,128]{1,0:T(8,128)}, f32[192,128]{1,0:T(8,128)}) custom-call(f32[4]{0:T(128)} %coef.1, f32[144,128]{1,0:T(8,128)} %bitcast.10, f32[144,128]{1,0:T(8,128)} %bitcast.11, f32[192,128]{1,0:T(8,128)} %bitcast.7), custom_call_target="tpu_custom_call" | custom-call | tf_op jit(solution)/shard_map/pallas_call | solution.py:618
  36.5 0.0 copy-start.1
  36.5 1.6 %copy.13 = f32[4,3,3,2,1,1,256]{6,5,4,3,2,1,0:T(1,128)} copy(f32[4,3,3,2,1,1,256]{6,5,4,3,2,1,0:T(1,128)} %bitcast.9) | data formatting | bytes 147456
  38.0 0.0 copy-done.1
  38.0 0.0 copy-start
  38.0 0.6 %copy.14 = f32[4,3,3,2,1,1,256]{6,5,4,3,2,1,0:T(1,128)} copy(f32[4,3,3,2,1,1,256]{6,5,4,3,2,1,0:T(1,128)S(1)} %bitcast.8) | data formatting | bytes 147456
  38.7 0.3 copy-done
  38.9 0.6 %copy.15 = f32[8,3,2,2,1,1,256]{6,5,4,3,2,1,0:T(1,128)} copy(f32[8,3,2,2,1,1,256]{6,5,4,3,2,1,0:T(1,128)S(1)} %bitcast.6) | data formatting | bytes 196608
Async XLA Ops:
  36.5 1.6 %copy-start.1 = (f32[144,128]{1,0:T(8,128)S(1)}, f32[144,128]{1,0:T(8,128)}, u32[]{:S(2)}) copy-start(f32[144,128]{1,0:T(8,128)} %get-tuple-element.7) | copy-start | bytes 221188
  38.0 0.9 %copy-start = (f32[192,128]{1,0:T(8,128)S(1)}, f32[192,128]{1,0:T(8,128)}, u32[]{:S(2)}) copy-start(f32[192,128]{1,0:T(8,128)} %get-tuple-element.8) | copy-start | bytes 294916

commit v2 on v1

--- a/solution.py
+++ b/solution.py
@@ -388,7 +388,6 @@
                     out_recv + slot,
                 )
                 moves.append((here, made))
-                pl.when(jnp.logical_not(here))(made.start)
 
         @pl.when(own_tile == grp)
         def _():
@@ -445,15 +444,19 @@
             state[6, :, 2] = third_row(got_u[4])
             last[0].wait_recv()
             state[6] = evolve(got_p[0, 4], state[6])
-        for one in made:
+        for i, one in ((0, made[2]), (2, made[3])):
             one.wait_recv()
-
-        @pl.loop(0, 4)
-        def _(i):
             state[i + 1] = evolve(got_p[r, i], state[i + 1])
-
+        for one in made[4:]:
+            one.wait_recv()
         low, high = got_pair_p[r, 0], got_pair_p[r, 1]
         state[5] = evolve(jnp.concatenate([low, high, high, high], axis=1), state[5])
+        for i, one in ((1, made[0]), (3, made[1])):
+            one.wait_recv()
+            state[i + 1] = evolve(got_p[r, i], state[i + 1])
+        if ring and r == 0:
+            for here, one in moves:
+                pl.when(jnp.logical_not(here))(one.start)
         if r + 1 < NSTEP:
             moment = moment - time_step * force()
 
@@ -500,9 +503,6 @@
     if ring:
         for at, slot in ((0, 0), (1, 2), (3, 4)):
             store_links(at, slot)
-        last[1].wait_recv()
-        state[6] = evolve(got_p[1, 4], state[6])
-        store_links(2, 6)
         for slot in range(n_x):
             waiter = describe(v_in.at[0, 0], fields.at[0, slot], beside(1, 0), 0, out_recv + slot)
             if slot:
@@ -511,21 +511,19 @@
                 pl.when(own_tile != grp)(waiter.wait_recv)
 
         def hop(k, g):
-            after, before = (g + 1) % n_x, (g + n_x - 1) % n_x
+            after, before = lax.rem(g + 1, n_x), lax.rem(g + n_x - 1, n_x)
             acc = hop_local(k, g, g)
             acc = acc + matvec(hop_links[g, 0], fields[k, after])
             acc = acc + matvec(hop_links[before, 0], fields[k, before], True)
             step(k, g, acc)
 
-        for k in range(NCHEB - 1):
-
-            @pl.loop(0, n_x)
-            def _(g):
-                after, before = lax.rem(g + 1, n_x), lax.rem(g + n_x - 1, n_x)
-                acc = hop_local(k, g, g)
-                acc = acc + matvec(hop_links[g, 0], fields[k, after])
-                acc = acc + matvec(hop_links[before, 0], fields[k, before], True)
-                step(k, g, acc)
+        pl.loop(0, 2)(functools.partial(hop, 0))
+        last[1].wait_recv()
+        state[6] = evolve(got_p[1, 4], state[6])
+        store_links(2, 6)
+        pl.loop(2, n_x)(functools.partial(hop, 0))
+        for k in range(1, NCHEB - 1):
+            pl.loop(0, n_x)(functools.partial(hop, k))
 
         back_send, back_recv = take(n_x), take(2 * tiles)
         backs = []
@@ -606,6 +604,17 @@
         one.wait_send()
 
 
+def leave(*refs):
+    sem = refs[-1]
+    copies = [
+        pltpu.make_async_copy(refs[n], refs[n + 3], sem.at[n]) for n in range(3)
+    ]
+    for one in copies:
+        one.start()
+    for one in copies:
+        one.wait()
+
+
 def body(sizes, links, momenta, vectors, coefficients):
     tiles = vectors.shape[0] * 2 // ROWS
     groups = 2 * tiles
@@ -618,9 +627,9 @@
     new_links, new_momenta, filtered = pl.pallas_call(
         functools.partial(kernel, sizes, tiles),
         out_shape=(
-            jax.ShapeDtypeStruct(flat_links, F32),
-            jax.ShapeDtypeStruct(flat_links, F32),
-            jax.ShapeDtypeStruct(flat_vectors, F32),
+            pltpu.VMEM(flat_links, F32),
+            pltpu.VMEM(flat_links, F32),
+            pltpu.VMEM(flat_vectors, F32),
         ),
         in_specs=[pl.BlockSpec(memory_space=pltpu.SMEM)] + [hbm] * 3,
         out_specs=(vmem,) * 3,
@@ -657,6 +666,17 @@
         momenta.reshape(flat_links),
         vectors.reshape(flat_vectors),
     )
+    new_links, new_momenta, filtered = pl.pallas_call(
+        leave,
+        out_shape=(
+            jax.ShapeDtypeStruct(flat_links, F32),
+            jax.ShapeDtypeStruct(flat_links, F32),
+            jax.ShapeDtypeStruct(flat_vectors, F32),
+        ),
+        in_specs=[vmem] * 3,
+        out_specs=(hbm,) * 3,
+        scratch_shapes=[pltpu.SemaphoreType.DMA((3,))],
+    )(new_links, new_momenta, filtered)
     return (
         new_links.reshape(links.shape),
         new_momenta.reshape(momenta.shape),

time: 39.8 us -> 38.4 us (0.965)
  local copies, waits for them, and re-layouts: 3.12 us -> 1.88 us
    unnamed x7 -> x6, local copies, waits for them, and re-layouts: 3.12 us -> 1.88 us
    pallas_call x1 -> x2, Pallas kernels: 35.8 us -> 35.7 us  [the longest x1 34 us: body(): pl.pallas_call(functools.partial(kernel, sizes, tiles), out_shape=(pltpu....]
where the time goes in v2:
time: 38.4 us; the launch traced here: 38.2 us
  Pallas kernels  35.7 us (93%)
  local copies, waits for them, and re-layouts  1.88 us (5%)
  between operations  0.65 us (2%)
    pallas_call x1, Pallas kernels, body(): pl.pallas_call(functools.partial(kernel, sizes, tiles), out_shape=(pltpu....  34 us
    unnamed x6, local copies, waits for them, and re-layouts  1.88 us
    pallas_call x1, Pallas kernels, body(): pl.pallas_call(leave, out_shape=(jax.ShapeDtypeStruct(flat_links, F32), j...  1.68 us

profile of v2, /device:TPU:0, one launch (start us, length us, event | category | flops | bytes accessed | tf_op | source)
XLA Modules:
  0.0 38.2 jit_solution(5610736515948354687)
XLA Ops:
  0.6 34.0 %shard_map.67 = (f32[144,128]{1,0:T(8,128)S(1)}, f32[144,128]{1,0:T(8,128)S(1)}, f32[192,128]{1,0:T(8,128)S(1)}) custom-call(f32[4]{0:T(128)} %coef.1, f32[144,128]{1,0:T(8,128)} %bitcast.7, f32[144,128]{1,0:T(8,128)} %bitcast.8, f32[192,128]{1,0:T(8,128)} %bitcast.6), custom_call_target="tpu_custom_call" | custom-call | tf_op jit(solution)/shard_map/pallas_call | solution.py:627
  34.7 0.0 copy-start
  34.7 0.6 %copy-done = f32[192,128]{1,0:T(8,128)} copy-done((f32[192,128]{1,0:T(8,128)}, f32[192,128]{1,0:T(8,128)S(1)}, u32[]{:S(2)}) %copy-start) | copy-done | bytes 98328
  35.3 0.0 copy-start.1
  35.3 0.6 %copy-done.1 = f32[144,128]{1,0:T(8,128)} copy-done((f32[144,128]{1,0:T(8,128)}, f32[144,128]{1,0:T(8,128)S(1)}, u32[]{:S(2)}) %copy-start.1) | copy-done | bytes 73752
  35.9 0.0 copy-start.2
  35.9 0.6 %copy-done.2 = f32[144,128]{1,0:T(8,128)} copy-done((f32[144,128]{1,0:T(8,128)}, f32[144,128]{1,0:T(8,128)S(1)}, u32[]{:S(2)}) %copy-start.2) | copy-done | bytes 73752
  36.5 1.7 %shard_map.68 = (f32[144,128]{1,0:T(8,128)}, f32[144,128]{1,0:T(8,128)}, f32[192,128]{1,0:T(8,128)}) custom-call(f32[144,128]{1,0:T(8,128)} %copy-done.1, f32[144,128]{1,0:T(8,128)} %copy-done.2, f32[192,128]{1,0:T(8,128)} %copy-done), custom_call_target="tpu_custom_call" | custom-call | tf_op jit(solution)/shard_map/pallas_call | solution.py:669
Async XLA Ops:
  34.7 0.6 %copy-start = (f32[192,128]{1,0:T(8,128)}, f32[192,128]{1,0:T(8,128)S(1)}, u32[]{:S(2)}) copy-start(f32[192,128]{1,0:T(8,128)S(1)} %get-tuple-element.11.refs_2_) | copy-start | bytes 294916
  35.3 0.6 %copy-start.1 = (f32[144,128]{1,0:T(8,128)}, f32[144,128]{1,0:T(8,128)S(1)}, u32[]{:S(2)}) copy-start(f32[144,128]{1,0:T(8,128)S(1)} %get-tuple-element.9.refs_0_) | copy-start | bytes 221188
  35.9 0.6 %copy-start.2 = (f32[144,128]{1,0:T(8,128)}, f32[144,128]{1,0:T(8,128)S(1)}, u32[]{:S(2)}) copy-start(f32[144,128]{1,0:T(8,128)S(1)} %get-tuple-element.10.refs_1_) | copy-start | bytes 221188

commit v3 on v2

--- a/solution.py
+++ b/solution.py
@@ -20,8 +20,16 @@
 UPPER = ((0, 1), (0, 2), (1, 2))
 
 
-def iota(shape, dim):
-    return lax.broadcasted_iota(jnp.int32, shape, len(shape) + dim)
+def rows_of():
+    return lax.broadcasted_iota(jnp.int32, (ROWS, LANES), 0)
+
+
+def lanes_of():
+    return lax.broadcasted_iota(jnp.int32, (ROWS, LANES), 1)
+
+
+def choose(mask, first, second):
+    return jnp.where(jnp.broadcast_to(mask, first.shape), first, second)
 
 
 def row_roll(values, count):
@@ -33,33 +41,32 @@
 
 def swap_halves(values):
     axis = values.ndim - 2
-    return jnp.where(
-        iota(values.shape, -2) % 2 == 0,
+    return choose(
+        (rows_of() & 1) == 0,
         pltpu.roll(values, ROWS - 1, axis=axis),
         pltpu.roll(values, 1, axis=axis),
     )
 
 
 def roll_y(values, amount):
-    lane = iota(values.shape, -1)
     axis = values.ndim - 1
     if amount == 1:
         moved = pltpu.roll(values, LANES - NZ, axis=axis)
-        return jnp.where(lane < LANES - NZ, moved, swap_halves(moved))
+        return choose(lanes_of() < LANES - NZ, moved, swap_halves(moved))
     moved = pltpu.roll(values, NZ, axis=axis)
-    return jnp.where(lane >= NZ, moved, swap_halves(moved))
+    return choose(lanes_of() >= NZ, moved, swap_halves(moved))
 
 
 def roll_z(values, amount):
-    position = iota(values.shape, -1) % NZ
+    position = lanes_of() & (NZ - 1)
     axis = values.ndim - 1
     if amount == 1:
-        return jnp.where(
+        return choose(
             position == NZ - 1,
             pltpu.roll(values, NZ - 1, axis=axis),
             pltpu.roll(values, LANES - 1, axis=axis),
         )
-    return jnp.where(
+    return choose(
         position == 0,
         pltpu.roll(values, LANES - NZ + 1, axis=axis),
         pltpu.roll(values, 1, axis=axis),
@@ -67,12 +74,9 @@
 
 
 def by_pair(choices):
-    row = iota(choices[0].shape, -2)
-    return jnp.where(
-        row < 4,
-        jnp.where(row < 2, choices[0], choices[1]),
-        jnp.where(row < 6, choices[2], choices[3]),
-    )
+    row = rows_of()
+    low = choices[0] if choices[0] is choices[1] else choose(row < 2, choices[0], choices[1])
+    return choose(row < 4, low, choose(row < 6, choices[2], choices[3]))
 
 
 def product(left, right, left_h=False, right_h=False):
@@ -201,7 +205,10 @@
 
 
 def spread(values, pair):
-    return by_pair([row_roll(values, pair - p) for p in range(4)])
+    row = rows_of()
+    step = -1 if pair % 2 == 0 else 1
+    values = choose((row & 2) == 2 * (pair % 2), values, row_roll(values, step))
+    return choose((row & 4) == 4 * (pair // 2), values, row_roll(values, 2))
 
 
 def matvec(matrix, v, herm=False):
@@ -313,6 +320,11 @@
     ]
     for load in loads:
         load.start()
+    stores = [
+        pltpu.make_async_copy(links_in, links_out, load_sem.at[3]),
+        pltpu.make_async_copy(momenta_in, momenta_out, load_sem.at[4]),
+        pltpu.make_async_copy(vectors_in, vectors_out, load_sem.at[5]),
+    ]
 
     counter = [0]
 
@@ -464,19 +476,21 @@
         done = moment - (0.5 * time_step) * force()
         zero = jnp.zeros_like(done[0])
         for n, (i, j) in enumerate(UPPER):
-            scatter_rows(momenta_out, link_rows(i, j, 0), done[n])
-            scatter_rows(momenta_out, link_rows(j, i, 0), -done[n])
-            scatter_rows(momenta_out, link_rows(i, j, 1), done[n + 3])
-            scatter_rows(momenta_out, link_rows(j, i, 1), done[n + 3])
+            scatter_rows(momenta_in, link_rows(i, j, 0), done[n])
+            scatter_rows(momenta_in, link_rows(j, i, 0), -done[n])
+            scatter_rows(momenta_in, link_rows(i, j, 1), done[n + 3])
+            scatter_rows(momenta_in, link_rows(j, i, 1), done[n + 3])
         for i in range(3):
-            scatter_rows(momenta_out, link_rows(i, i, 0), zero)
-            scatter_rows(momenta_out, link_rows(i, i, 1), done[6 + i])
+            scatter_rows(momenta_in, link_rows(i, i, 0), zero)
+            scatter_rows(momenta_in, link_rows(i, i, 1), done[6 + i])
+        stores[1].start()
 
     def finish_links():
         for i in range(3):
             for j in range(3):
                 for c in range(2):
-                    scatter_rows(links_out, link_rows(i, j, c), state[0, c, i, j])
+                    scatter_rows(links_in, link_rows(i, j, c), state[0, c, i, j])
+        stores[0].start()
 
     def step(k, g, acc):
         acc = acc * (-1.0 / 6.0)
@@ -546,8 +560,8 @@
         def _():
             v_done[grp, home] = total[0]
 
+        finish_links()
         finish_momenta()
-        finish_links()
         for h in range(2):
             for tile in range(tiles):
                 here, _ = moves[h * tiles + tile]
@@ -599,9 +613,12 @@
         for tile in range(tiles):
             for c in range(2):
                 for a in range(3):
-                    scatter_rows(vectors_out, vector_rows(tile, a, c, h), v_done[h, tile, c, a])
+                    scatter_rows(vectors_in, vector_rows(tile, a, c, h), v_done[h, tile, c, a])
+    stores[2].start()
     for one in pending:
         one.wait_send()
+    for one in stores:
+        one.wait()
 
 
 def leave(*refs):
@@ -619,7 +636,6 @@
     tiles = vectors.shape[0] * 2 // ROWS
     groups = 2 * tiles
     copies = 2 * (groups + 4) + 7 + 7 * NSTEP + 2 * NCHEB + 2
-    vmem = pl.BlockSpec(memory_space=pltpu.VMEM)
     hbm = pl.BlockSpec(memory_space=pltpu.HBM)
     tile = (ROWS, LANES)
     flat_links = (links.size // LANES, LANES)
@@ -627,12 +643,12 @@
     new_links, new_momenta, filtered = pl.pallas_call(
         functools.partial(kernel, sizes, tiles),
         out_shape=(
-            pltpu.VMEM(flat_links, F32),
-            pltpu.VMEM(flat_links, F32),
-            pltpu.VMEM(flat_vectors, F32),
+            jax.ShapeDtypeStruct(flat_links, F32),
+            jax.ShapeDtypeStruct(flat_links, F32),
+            jax.ShapeDtypeStruct(flat_vectors, F32),
         ),
         in_specs=[pl.BlockSpec(memory_space=pltpu.SMEM)] + [hbm] * 3,
-        out_specs=(vmem,) * 3,
+        out_specs=(hbm,) * 3,
         scratch_shapes=[
             pltpu.VMEM(flat_links, F32),
             pltpu.VMEM(flat_links, F32),
@@ -653,7 +669,7 @@
             pltpu.VMEM((NCHEB, 2, groups, 2, 3) + tile, F32),
             pltpu.VMEM((groups, 2, 3) + tile, F32),
             pltpu.VMEM((groups, 2, 3) + tile, F32),
-            pltpu.SemaphoreType.DMA((3,)),
+            pltpu.SemaphoreType.DMA((6,)),
             pltpu.SemaphoreType.DMA((copies,)),
             pltpu.SemaphoreType.DMA((copies,)),
         ],
@@ -673,9 +689,10 @@
             jax.ShapeDtypeStruct(flat_links, F32),
             jax.ShapeDtypeStruct(flat_vectors, F32),
         ),
-        in_specs=[vmem] * 3,
+        in_specs=[hbm] * 3,
         out_specs=(hbm,) * 3,
         scratch_shapes=[pltpu.SemaphoreType.DMA((3,))],
+        compiler_params=pltpu.CompilerParams(vmem_limit_bytes=60 * 1024 * 1024),
     )(new_links, new_momenta, filtered)
     return (
         new_links.reshape(links.shape),

time: 38.4 us -> 44 us (1.15)
  Pallas kernels: 35.7 us -> 43.2 us
  local copies, waits for them, and re-layouts: 1.88 us -> 0 us
    pallas_call x1, Pallas kernels: 1.68 us -> 8.58 us  [body(): pl.pallas_call(leave, out_shape=(jax.ShapeDtypeStruct(flat_links, F32), j...]
    unnamed x6 -> x0, local copies, waits for them, and re-layouts: 1.88 us -> none
    pallas_call x1, Pallas kernels: 34 us -> 34.7 us  [body(): pl.pallas_call(functools.partial(kernel, sizes, tiles), out_shape=(jax.Sh...]
where the time goes in v3:
time: 44 us; the launch traced here: 43.9 us
  Pallas kernels  43.2 us (98%)
  between operations  0.64 us (1%)
    pallas_call x1, Pallas kernels, body(): pl.pallas_call(functools.partial(kernel, sizes, tiles), out_shape=(jax.Sh...  34.7 us
    pallas_call x1, Pallas kernels, body(): pl.pallas_call(leave, out_shape=(jax.ShapeDtypeStruct(flat_links, F32), j...  8.58 us

profile of v3, /device:TPU:0, one launch (start us, length us, event | category | flops | bytes accessed | tf_op | source)
XLA Modules:
  0.0 43.9 jit_solution(14147037472379422045)
XLA Ops:
  0.6 34.7 %shard_map.67 = (f32[144,128]{1,0:T(8,128)}, f32[144,128]{1,0:T(8,128)}, f32[192,128]{1,0:T(8,128)}) custom-call(f32[4]{0:T(128)} %coef.1, f32[144,128]{1,0:T(8,128)} %bitcast.7, f32[144,128]{1,0:T(8,128)} %bitcast.8, f32[192,128]{1,0:T(8,128)} %bitcast.6), custom_call_target="tpu_custom_call" | custom-call | tf_op jit(solution)/shard_map/pallas_call | solution.py:643
  35.3 8.6 %shard_map.68 = (f32[144,128]{1,0:T(8,128)}, f32[144,128]{1,0:T(8,128)}, f32[192,128]{1,0:T(8,128)}) custom-call(f32[144,128]{1,0:T(8,128)} %get-tuple-element.9.refs_0_, f32[144,128]{1,0:T(8,128)} %get-tuple-element.10.refs_1_, f32[192,128]{1,0:T(8,128)} %get-tuple-element.11.refs_2_), custom_call_target="tpu_custom_call" | custom-call | tf_op jit(solution)/shard_map/pallas_call | solution.py:685

commit v4 on v3

--- a/solution.py
+++ b/solution.py
@@ -278,6 +278,8 @@
     pair_p,
     got_p,
     got_pair_p,
+    far_u,
+    got_far,
     hop_links,
     fields,
     got_fields,
@@ -381,8 +383,6 @@
         made.wait_recv()
 
     if ring:
-        far = copy(two_rows, got_u.at[4], whole_to[4])
-        pending.append(far)
         own_tile = x // tiles
         home = lax.rem(x, tiles)
         out_send, out_recv = take(2 * tiles), take(n_x)
@@ -427,8 +427,6 @@
         pair_p[r, 1] = moment[:, 2:4, :]
         made = [copy(send_p.at[r], got_p.at[r, i], whole_to[i]) for i in (1, 3, 0, 2)]
         made += [copy(pair_p.at[r, i], got_pair_p.at[r, i], pair_to[i]) for i in range(2)]
-        if ring:
-            made.append(copy(send_p.at[r], got_p.at[r, 4], whole_to[4]))
         return made
 
     def send_fields(r):
@@ -438,24 +436,26 @@
         ]
 
     halo = None
-    last = []
+    entries = [(c, i, j) for c in range(2) for i in range(3) for j in range(3)]
+
+    def far_rows(n):
+        return [2 * (len(entries) * d + n) for d in range(3)]
+
     moment = send_p[0] - (0.5 * time_step) * force()
     for r in range(NSTEP):
         made = send_moment(r, moment)
         pending += made
-        if ring:
-            last.append(made.pop())
-        elif r == 0:
+        if r == 0 and not ring:
             give.wait_recv()
             halo = send_fields(0)
             pending += halo
         state[0] = evolve(moment, state[0])
-        if ring and r == 1:
-            far.wait_recv()
-            state[6, :, 0:2] = got_u[4]
-            state[6, :, 2] = third_row(got_u[4])
-            last[0].wait_recv()
-            state[6] = evolve(got_p[0, 4], state[6])
+        if ring and r + 1 == NSTEP:
+            for n, (c, i, j) in enumerate(entries):
+                scatter_rows(far_u, far_rows(n), state[0, c, i, j][2:])
+            far_u[pl.ds(6 * len(entries), 4), :] = jnp.zeros((4, LANES), F32)
+            far = copy(far_u, got_far, whole_to[4])
+            pending.append(far)
         for i, one in ((0, made[2]), (2, made[3])):
             one.wait_recv()
             state[i + 1] = evolve(got_p[r, i], state[i + 1])
@@ -532,8 +532,10 @@
             step(k, g, acc)
 
         pl.loop(0, 2)(functools.partial(hop, 0))
-        last[1].wait_recv()
-        state[6] = evolve(got_p[1, 4], state[6])
+        far.wait_recv()
+        for n, (c, i, j) in enumerate(entries):
+            starts = far_rows(n)
+            state[6, c, i, j] = gather_rows(got_far, starts[:1] + starts)
         store_links(2, 6)
         pl.loop(2, n_x)(functools.partial(hop, 0))
         for k in range(1, NCHEB - 1):
@@ -622,13 +624,15 @@
 
 
 def leave(*refs):
-    sem = refs[-1]
-    copies = [
-        pltpu.make_async_copy(refs[n], refs[n + 3], sem.at[n]) for n in range(3)
-    ]
-    for one in copies:
+    ins, outs, held, sem = refs[0:3], refs[3:6], refs[6:9], refs[9]
+    loads = [pltpu.make_async_copy(ins[n], held[n], sem.at[n]) for n in range(3)]
+    stores = [pltpu.make_async_copy(held[n], outs[n], sem.at[n + 3]) for n in range(3)]
+    for one in loads:
         one.start()
-    for one in copies:
+    for load, store in zip(loads, stores):
+        load.wait()
+        store.start()
+    for one in stores:
         one.wait()
 
 
@@ -658,12 +662,14 @@
             pltpu.VMEM((2, tiles, 2, 3) + tile, F32),
             pltpu.VMEM((7, 2, 3, 3) + tile, F32),
             pltpu.VMEM((2, 2, 2, 3, 2, LANES), F32),
-            pltpu.VMEM((5, 2, 2, 3) + tile, F32),
+            pltpu.VMEM((4, 2, 2, 3) + tile, F32),
             pltpu.VMEM((2, 2, 2, 3, 2, LANES), F32),
             pltpu.VMEM((NSTEP, 9) + tile, F32),
             pltpu.VMEM((NSTEP, 2, 9, 2, LANES), F32),
-            pltpu.VMEM((NSTEP, 5, 9) + tile, F32),
+            pltpu.VMEM((NSTEP, 4, 9) + tile, F32),
             pltpu.VMEM((NSTEP, 2, 9, 2, LANES), F32),
+            pltpu.VMEM((112, LANES), F32),
+            pltpu.VMEM((112, LANES), F32),
             pltpu.VMEM((4, 5, 2, 3, 3) + tile, F32),
             pltpu.VMEM((NCHEB, groups, 2, 3) + tile, F32),
             pltpu.VMEM((NCHEB, 2, groups, 2, 3) + tile, F32),
@@ -691,7 +697,12 @@
         ),
         in_specs=[hbm] * 3,
         out_specs=(hbm,) * 3,
-        scratch_shapes=[pltpu.SemaphoreType.DMA((3,))],
+        scratch_shapes=[
+            pltpu.VMEM(flat_links, F32),
+            pltpu.VMEM(flat_links, F32),
+            pltpu.VMEM(flat_vectors, F32),
+            pltpu.SemaphoreType.DMA((6,)),
+        ],
         compiler_params=pltpu.CompilerParams(vmem_limit_bytes=60 * 1024 * 1024),
     )(new_links, new_momenta, filtered)
     return (

time: 44 us -> 36.1 us (0.82)
  Pallas kernels: 43.2 us -> 35.2 us
    pallas_call x1, Pallas kernels: 8.58 us -> 1.66 us  [body(): pl.pallas_call(leave, out_shape=(jax.ShapeDtypeStruct(flat_links, F32), j...]
    pallas_call x1, Pallas kernels: 34.7 us -> 33.6 us  [body(): pl.pallas_call(functools.partial(kernel, sizes, tiles), out_shape=(jax.Sh...]
where the time goes in v4:
time: 36.1 us; the launch traced here: 35.9 us
  Pallas kernels  35.2 us (98%)
  between operations  0.64 us (2%)
    pallas_call x1, Pallas kernels, body(): pl.pallas_call(functools.partial(kernel, sizes, tiles), out_shape=(jax.Sh...  33.6 us
    pallas_call x1, Pallas kernels, body(): pl.pallas_call(leave, out_shape=(jax.ShapeDtypeStruct(flat_links, F32), j...  1.66 us

profile of v4, /device:TPU:0, one launch (start us, length us, event | category | flops | bytes accessed | tf_op | source)
XLA Modules:
  0.0 35.9 jit_solution(11870083060952033451)
XLA Ops:
  0.6 33.6 %shard_map.67 = (f32[144,128]{1,0:T(8,128)}, f32[144,128]{1,0:T(8,128)}, f32[192,128]{1,0:T(8,128)}) custom-call(f32[4]{0:T(128)} %coef.1, f32[144,128]{1,0:T(8,128)} %bitcast.7, f32[144,128]{1,0:T(8,128)} %bitcast.8, f32[192,128]{1,0:T(8,128)} %bitcast.6), custom_call_target="tpu_custom_call" | custom-call | tf_op jit(solution)/shard_map/pallas_call | solution.py:647
  34.2 1.7 %shard_map.68 = (f32[144,128]{1,0:T(8,128)}, f32[144,128]{1,0:T(8,128)}, f32[192,128]{1,0:T(8,128)}) custom-call(f32[144,128]{1,0:T(8,128)} %get-tuple-element.9.refs_0_, f32[144,128]{1,0:T(8,128)} %get-tuple-element.10.refs_1_, f32[192,128]{1,0:T(8,128)} %get-tuple-element.11.refs_2_), custom_call_target="tpu_custom_call" | custom-call | tf_op jit(solution)/shard_map/pallas_call | solution.py:691

commit v5 on v4

--- a/solution.py
+++ b/solution.py
@@ -463,12 +463,13 @@
             one.wait_recv()
         low, high = got_pair_p[r, 0], got_pair_p[r, 1]
         state[5] = evolve(jnp.concatenate([low, high, high, high], axis=1), state[5])
-        for i, one in ((1, made[0]), (3, made[1])):
-            one.wait_recv()
-            state[i + 1] = evolve(got_p[r, i], state[i + 1])
+        made[0].wait_recv()
+        made[1].wait_recv()
         if ring and r == 0:
             for here, one in moves:
                 pl.when(jnp.logical_not(here))(one.start)
+        for i in (1, 3):
+            state[i + 1] = evolve(got_p[r, i], state[i + 1])
         if r + 1 < NSTEP:
             moment = moment - time_step * force()
 

time: 36.1 us -> 36.2 us (level)
  no operation moved by 1% of the time
where the time goes in v5:
time: 36.2 us; the launch traced here: 36 us
  Pallas kernels  35.4 us (98%)
  between operations  0.64 us (2%)
    pallas_call x1, Pallas kernels, body(): pl.pallas_call(functools.partial(kernel, sizes, tiles), out_shape=(jax.Sh...  33.7 us
    pallas_call x1, Pallas kernels, body(): pl.pallas_call(leave, out_shape=(jax.ShapeDtypeStruct(flat_links, F32), j...  1.66 us

profile of v5, /device:TPU:0, one launch (start us, length us, event | category | flops | bytes accessed | tf_op | source)
XLA Modules:
  0.0 36.0 jit_solution(11375452170735737809)
XLA Ops:
  0.6 33.7 %shard_map.67 = (f32[144,128]{1,0:T(8,128)}, f32[144,128]{1,0:T(8,128)}, f32[192,128]{1,0:T(8,128)}) custom-call(f32[4]{0:T(128)} %coef.1, f32[144,128]{1,0:T(8,128)} %bitcast.7, f32[144,128]{1,0:T(8,128)} %bitcast.8, f32[192,128]{1,0:T(8,128)} %bitcast.6), custom_call_target="tpu_custom_call" | custom-call | tf_op jit(solution)/shard_map/pallas_call | solution.py:648
  34.4 1.7 %shard_map.68 = (f32[144,128]{1,0:T(8,128)}, f32[144,128]{1,0:T(8,128)}, f32[192,128]{1,0:T(8,128)}) custom-call(f32[144,128]{1,0:T(8,128)} %get-tuple-element.9.refs_0_, f32[144,128]{1,0:T(8,128)} %get-tuple-element.10.refs_1_, f32[192,128]{1,0:T(8,128)} %get-tuple-element.11.refs_2_), custom_call_target="tpu_custom_call" | custom-call | tf_op jit(solution)/shard_map/pallas_call | solution.py:692
